TPU v7x, 32 devices: a whole 2x2x4 slice. The times are simulated.
32 devices in a mesh: head: 1, seq: 32 (over z, y, x, core).
Axes of the slice: x: 2, y: 2, z: 4, core: 2. Of those that a mesh axis runs over, the one named last changes fastest.
Arguments:
- query_rows: bfloat16 [8, 16384, 512], P('head', 'seq'), may hold values from -16 to 16
- key_rows: bfloat16 [8, 16384, 512], P('head', 'seq'), may hold values from -16 to 16
- value_rows: bfloat16 [8, 16384, 512], P('head', 'seq'), may hold values from -6 to 6
- step_rate: float32 [8, 16384], P('head', 'seq'), may hold values from 0.15 to 162
- doc_start: int32 [16384], P('seq'), may hold values from 0 to 16383, as said below
- speech_flag: int32 [16384], P('seq'), may hold values 0 or 1
- w_gate: bfloat16 [8, 512, 512], P('head'), may hold values from -0.25 to 0.25
- w_up: bfloat16 [8, 512, 512], P('head'), may hold values from -0.25 to 0.25
- w_down: bfloat16 [8, 512, 512], P('head'), may hold values from -0.25 to 0.25
- w_cond: bfloat16 [4096, 512], P('head'), may hold values from -0.09375 to 0.09375
Outputs:
- mixed: bfloat16 [8, 16384, 512], P('head', 'seq')
- cond: bfloat16 [32, 512, 512], P('seq', 'head')
Inputs may be any that keep to these rules, and one draw needn't show every extreme that they name: doc_start[p] is the position of the first token of the document holding token p: at most p, never falling along the sequence, and doc_start[q] = q wherever a document begins; the last token begins a document of its own.
All inputs are finite; a program needn't handle non-finite values. No bound on the sum of `speech_flag` on one device may be relied on, other than what follows from the above.
Results may differ from a plain program's by a relative error of at most 0.015.
Values may be sent and summed in bfloat16 or wider, within the bound.
A program may use at most 128 MiB of HBM per device.

v0:
```python
import math

import jax
import jax.numpy as jnp
from jax import lax
from jax.sharding import PartitionSpec as P

WIN = 512


eps_norm = 1e-06


def passed_along(block, axis, distance):
    devices = range(lax.axis_size(axis))
    route = [(i - distance, i) for i in devices if i - distance in devices]
    return lax.ppermute(block, axis, route)


def renorm_rows(old_rows, summed, factor):
    old_f = old_rows.astype(jnp.float32)
    updated = old_f + summed * factor[None, :, None, None]
    old_norm = jnp.sqrt(jnp.sum(old_f * old_f, axis=-1, keepdims=True))
    new_norm = jnp.sqrt(jnp.sum(updated * updated, axis=-1, keepdims=True) + eps_norm)
    return (updated * (old_norm / new_norm)).astype(jnp.bfloat16)


def local(
    query_rows,
    key_rows,
    value_rows,
    step_rate,
    doc_start,
    speech_flag,
    w_gate,
    w_up,
    w_down,
    w_cond,
):
    head_local, tok_local, head_width = query_rows.shape
    cond_width = w_cond.shape[1]
    seq_count = lax.axis_size("seq")
    head_count = lax.axis_size("head")
    seq_index = lax.axis_index("seq")
    offset = seq_index * tok_local
    half_seq = seq_count // 2
    update_len = tok_local * half_seq
    in_first = seq_index < half_seq
    speech_on = speech_flag.astype(jnp.float32)
    prev_key, prev_value = passed_along((key_rows, value_rows), "seq", 1)
    keys_all = jnp.concatenate([prev_key, key_rows], axis=1)
    values_all = jnp.concatenate([prev_value, value_rows], axis=1)
    block_rows = min(512, tok_local)
    score_scale = 1.0 / math.sqrt(head_width)

    def attend(row_start):
        pos_query = offset + row_start + jnp.arange(block_rows, dtype=jnp.int32)
        pos_key = offset + row_start - WIN + jnp.arange(WIN + block_rows, dtype=jnp.int32)
        allowed = (
            (pos_key[None, :] <= pos_query[:, None])
            & (pos_key[None, :] > pos_query[:, None] - WIN)
            & (pos_key[None, :] >= doc_start[:, None])
        )
        scores = (
            jnp.einsum("hqd,hkd->hqk", query_rows, keys_all, preferred_element_type=jnp.float32)
            * score_scale
        )
        scores = jnp.where(allowed[None], scores, -1e30)
        row_max = jnp.max(scores, axis=-1, keepdims=True)
        expon = jnp.exp(scores - row_max)
        prob_bf = (expon / jnp.sum(expon, axis=-1, keepdims=True)).astype(jnp.bfloat16)
        return jnp.einsum("hqk,hkd->hqd", prob_bf, values_all, preferred_element_type=jnp.float32)

    blocks = lax.map(attend, jnp.arange(tok_local // block_rows, dtype=jnp.int32) * block_rows)
    attended = jnp.moveaxis(blocks, 0, 1).reshape(head_local, tok_local, head_width)
    first_mask = in_first.astype(jnp.float32)
    rate_local = jnp.sum(step_rate, axis=1) * first_mask
    token_mask = speech_on * first_mask
    scaled = (
        token_mask[None, :, None] * step_rate[:, :, None] * value_rows.astype(jnp.float32)
    ).astype(jnp.bfloat16)
    gate_pre = jnp.einsum("htd,hrd->htr", key_rows, w_gate, preferred_element_type=jnp.float32)
    up_pre = jnp.einsum("htd,hrd->htr", key_rows, w_up, preferred_element_type=jnp.float32)
    sigma = jax.nn.sigmoid(gate_pre)
    active = gate_pre * sigma
    hidden_zero = (active * up_pre).astype(jnp.bfloat16)
    back = jnp.einsum("htd,hdr->htr", scaled, w_down, preferred_element_type=jnp.float32)
    grad_gate = (back * up_pre * sigma * (1.0 + gate_pre * (1.0 - sigma))).astype(jnp.bfloat16)
    grad_up = (back * active).astype(jnp.bfloat16)
    w_zero = jnp.transpose(jnp.stack((w_gate, w_up, w_down), axis=2), (1, 0, 2, 3))
    unit_scale = jnp.ones((head_local,), jnp.float32)
    totals = lax.psum(rate_local, "seq")
    inner = 2.0 * update_len / (totals * math.sqrt(update_len * head_width))
    row_share = head_width // seq_count
    term_gate = jnp.einsum("htr,htd->rhd", grad_gate, key_rows, preferred_element_type=jnp.float32)
    term_up = jnp.einsum("htr,htd->rhd", grad_up, key_rows, preferred_element_type=jnp.float32)
    term_down = jnp.einsum("htr,htd->rhd", scaled, hidden_zero, preferred_element_type=jnp.float32)
    summed = lax.psum_scatter(
        jnp.stack((term_gate, term_up, term_down), axis=2) * inner[None, :, None, None],
        "seq",
        scatter_dimension=0,
        tiled=True,
    )
    old_rows = lax.dynamic_slice_in_dim(w_zero, seq_index * row_share, row_share, 0)
    fresh = lax.all_gather(renorm_rows(old_rows, summed, unit_scale), "seq", axis=0, tiled=True)
    chosen = jnp.where(in_first, w_zero, fresh)
    query_gate = jnp.einsum(
        "htd,rhd->htr", query_rows, chosen[:, :, 0], preferred_element_type=jnp.float32
    )
    query_up = jnp.einsum(
        "htd,rhd->htr", query_rows, chosen[:, :, 1], preferred_element_type=jnp.float32
    )
    query_hidden = (query_gate * jax.nn.sigmoid(query_gate) * query_up).astype(jnp.bfloat16)
    fast_out = jnp.einsum(
        "htr,dhr->htd", query_hidden, chosen[:, :, 2], preferred_element_type=jnp.float32
    )
    mixed = (attended + fast_out).astype(jnp.bfloat16)
    frame_rows = tok_local // head_count
    head_index = lax.axis_index("head")
    flag_rows = lax.dynamic_slice_in_dim(speech_on, head_index * frame_rows, frame_rows, 0)
    cond_weight = w_cond.reshape(head_local, head_width, cond_width)
    projected = lax.psum_scatter(
        jnp.einsum("htd,hdc->tc", mixed, cond_weight, preferred_element_type=jnp.float32).astype(
            jnp.bfloat16
        ),
        "head",
        scatter_dimension=0,
        tiled=True,
    ).astype(jnp.float32)
    cond = (projected * flag_rows[:, None]).astype(jnp.bfloat16)[None]
    return (mixed, cond)


def solution(mesh):
    placed = (
        P("head", "seq", None),
        P("head", "seq", None),
        P("head", "seq", None),
        P("head", "seq"),
        P("seq"),
        P("seq"),
        P("head", None, None),
        P("head", None, None),
        P("head", None, None),
        P("head", None),
    )
    return jax.shard_map(
        local,
        mesh=mesh,
        in_specs=placed,
        out_specs=(P("head", "seq", None), P("seq", "head", None)),
        check_vma=False,
    )
```

profile of v0, /device:TPU:24, one launch (start us, length us, event | category | flops | bytes accessed | tf_op | source)
XLA Modules:
  0.0 566.8 jit_solution(13197432284594158882)
XLA Ops:
  7.2 0.0 reduce-scatter.2.cloned.1.call-start
  7.2 0.0 copy-start.1
  7.2 0.0 copy-start.4
  7.2 9.2 %fusion.50 = f32[8,512,512]{2,1,0:T(8,128)} fusion(bf16[8,512,512]{2,1,0:T(8,128)(2,1)} %param.11, bf16[8,512,512]{2,1,0:T(8,128)(2,1)} %param.16), kind=kOutput, calls=%fused_computation.77 | convolution fusion | flops 2147483648 | bytes 16777216 | tf_op jit(solution)/shard_map/htd,hrd->htr/dot_general | solution.py:82
  16.4 0.0 copy-done.1
  16.4 0.0 copy-done.4
  16.4 0.0 copy-start.8
  16.4 0.0 copy-start.7
  16.5 0.0 copy-start
  16.5 0.0 copy-start.5
  16.5 5.6 fusion.49
  22.1 0.0 copy-done.8
  22.1 0.0 copy-done.7
  22.1 0.1 fusion.47
  22.2 0.0 copy-done
  22.2 0.0 copy-done.5
  22.2 2.8 fusion.25
  25.0 0.0 copy-start.2
  25.0 12.9 %fusion.28 = f32[512,8,1,512]{3,0,1,2:T(8,128)} fusion(bf16[8,512,512]{2,1,0:T(8,128)(2,1)S(1)} %copy-done.5, f32[8,512]{1,0:T(8,128)S(1)} %get-tuple-element.19, f32[8,512,512]{2,1,0:T(8,128)} %fusion.49, f32[8,512,512]{2,1,0:T(8,128)} %fusion.50), kind=kOutput, calls=%fused_computation.45 | convolution fusion | flops 2166358016 | bytes 29376512 | tf_op jit(solution)/shard_map/htr,htd->rhd/dot_general | solution.py:97
  37.9 0.0 copy-done.2
  37.9 12.6 %fusion.27 = f32[512,8,1,512]{3,0,1,2:T(8,128)} fusion(bf16[8,512,512]{2,1,0:T(8,128)(2,1)S(1)} %copy-done.4, f32[8,512,512]{2,1,0:T(8,128)} %fusion.50, f32[8,512,512]{2,1,0:T(8,128)S(1)} %fusion.25, f32[8,512,512]{2,1,0:T(8,128)} %fusion.49), kind=kOutput, calls=%fused_computation.44 | convolution fusion | flops 2168455168 | bytes 37748736 | tf_op jit(solution)/shard_map/htr,htd->rhd/dot_general | solution.py:95
  50.5 13.3 %fusion.26 = f32[512,8,1,512]{3,0,1,2:T(8,128)} fusion(bf16[8,512,512]{2,1,0:T(8,128)(2,1)} %param.11, f32[8,512,512]{2,1,0:T(8,128)} %copy-done.2, f32[8,512,512]{2,1,0:T(8,128)} %fusion.50), kind=kOutput, calls=%fused_computation.43 | convolution fusion | flops 2160066560 | bytes 29360128 | tf_op jit(solution)/shard_map/htr,htd->rhd/dot_general | solution.py:96
  63.8 39.1 %psum.7 = f32[8]{0:T(128)S(1)} all-reduce(f32[8]{0:T(128)S(1)} %broadcast_multiply_fusion.2), channel_id=1, replica_groups=mesh['head'=1,'seq'=32] {'seq'}, use_global_device_ids=true, to_apply=%region_3.4 | all-reduce | flops 8 | bytes 64 | tf_op jit(solution)/shard_map/psum | solution.py:92
  102.9 18.0 %maximum_multiply_fusion = f32[512,8,3,512]{3,0,1,2:T(8,128)} fusion(f32[512,8,1,512]{3,0,1,2:T(8,128)} %fusion.28, f32[512,8,1,512]{3,0,1,2:T(8,128)} %fusion.26, f32[512,8,1,512]{3,0,1,2:T(8,128)} %fusion.27, f32[8]{0:T(128)S(1)} %multiply_divide_fusion), kind=kLoop, calls=%fused_computation.1 | loop fusion | flops 18874368 | bytes 50331680 | tf_op jit(solution)/shard_map/mul | solution.py:99
  121.0 0.0 reduce-scatter.2.cloned.1.call-update
  121.0 0.0 all-gather.2.cloned.1.call-start
  121.0 0.0 copy-start.9
  121.0 10.7 %pad_maximum_fusion = bf16[8,512,3,512]{3,1,0,2:T(8,128)(2,1)} fusion(bf16[8,512,1,512]{3,1,0,2:T(8,128)(2,1)} %bitcast.96, bf16[8,512,1,512]{3,1,0,2:T(8,128)(2,1)} %bitcast.98, bf16[8,512,1,512]{3,1,0,2:T(8,128)(2,1)} %bitcast.100), kind=kLoop, calls=%fused_computation.6 | loop fusion | flops 12582912 | bytes 25165824 | tf_op jit(solution)/shard_map/stack | solution.py:90
  131.7 232.9 %reduce-scatter.2.cloned.1.call-done = f32[16,8,3,512]{3,0,1,2:T(8,128)} async-done(((f32[512,8,3,512]{3,0,1,2:T(8,128)}), f32[16,8,3,512]{3,0,1,2:T(8,128)}) %reduce-scatter.2.cloned.1.call-update) | async-done | bytes 786448 | tf_op jit(solution)/shard_map/reduce_scatter | solution.py:98
  364.6 1.5 fusion.38
  366.1 2.1 multiply_convert_fusion.17
  368.3 0.0 all-gather.2.cloned.1.call-update
  368.3 1.9 collective-permute-start
  370.2 3.7 collective-permute-start.1
  373.9 0.0 copy-done.9
  373.9 0.6 compare_and_fusion
  374.6 99.8 %collective-permute-done = bf16[8,512,512]{2,1,0:T(8,128)(2,1)} collective-permute-done((bf16[8,512,512]{2,1,0:T(8,128)(2,1)}, bf16[8,512,512]{2,1,0:T(8,128)(2,1)}, u32[]{:S(2)}, u32[]{:S(2)}) %collective-permute-start) | collective-permute-done | bytes 4194336 | tf_op jit(solution)/shard_map/ppermute | solution.py:17
  474.3 15.1 %fusion.2 = f32[8,1024,512]{2,1,0:T(8,128)} fusion(bf16[8,512,512]{2,1,0:T(8,128)(2,1)} %param.10, bf16[8,512,512]{2,1,0:T(8,128)(2,1)} %param.11, bf16[8,512,512]{2,1,0:T(8,128)(2,1)} %collective-permute-done), kind=kOutput, calls=%fused_computation.8 | convolution fusion | flops 4311744512 | bytes 29360128 | tf_op jit(solution)/shard_map/while/body/eval_jaxpr/hqd,hkd->hqk/dot_general | solution.py:65
  489.4 17.5 %fusion.48 = (f32[8,512]{1,0:T(8,128)S(1)}, f32[8,512,1024]{1,2,0:T(8,128)}) fusion(f32[8,1024,512]{2,1,0:T(8,128)} %fusion.2, pred[512,1024]{0,1:T(8,128)(4,1)S(1)} %compare_and_fusion), kind=kOutput, calls=%fused_computation.75 | output fusion | flops 25166848 | bytes 34095104 | tf_op jit(solution)/shard_map/while/body/eval_jaxpr/sub | solution.py:70
  507.0 0.0 all-gather.2.cloned.1.call-done
  507.0 0.0 copy-start.6
  507.0 9.4 %bitcast_select_fusion.4 = bf16[512,8,3,512]{3,0,1,2:T(8,128)(2,1)S(1)} fusion(bf16[512,8,3,512]{3,0,1,2:T(8,128)(2,1)} %all-gather.2.cloned.1.call-done, pred[]{:T(512)S(6)} %lt.8, bf16[8,512,1,512]{3,1,0,2:T(8,128)(2,1)} %bitcast.97, bf16[8,512,1,512]{3,1,0,2:T(8,128)(2,1)} %bitcast.99, bf16[8,512,1,512]{3,1,0,2:T(8,128)(2,1)} %bitcast.101), kind=kLoop, calls=%fused_computation.7 | loop fusion | flops 18874368 | bytes 37748736 | tf_op jit(solution)/shard_map/jit(_where)/select_n | solution.py:106
  516.4 0.0 copy-start.3
  516.4 4.5 copy-done.3
  520.9 0.0 copy-done.6
  520.9 5.6 fusion.21
  526.5 11.8 %fusion.20 = f32[8,512,512]{2,1,0:T(8,128)} fusion(bf16[512,8,3,512]{3,0,1,2:T(8,128)(2,1)} %copy-done.3, f32[8,512,512]{1,2,0:T(8,128)} %fusion.21, bf16[8,512,512]{2,1,0:T(8,128)(2,1)} %param.10), kind=kOutput, calls=%fused_computation.36 | convolution fusion | flops 4307550208 | bytes 29360128 | tf_op jit(solution)/shard_map/htr,dhr->htd/dot_general | solution.py:114
  538.3 0.0 collective-permute-done.1
  538.3 15.0 %add_convert_fusion = bf16[8,512,512]{2,1,0:T(8,128)(2,1)} fusion(f32[8,512,512]{2,1,0:T(8,128)} %fusion.20, bf16[8,512,512]{2,1,0:T(8,128)(2,1)} %param.12, bf16[8,512,512]{2,1,0:T(8,128)(2,1)} %collective-permute-done.1, f32[8,512,1024]{1,2,0:T(8,128)} %get-tuple-element.28, f32[8,512]{1,0:T(8,128)S(1)} %get-tuple-element.20), kind=kOutput, calls=%fused_computation.23 | convolution fusion | flops 4324327424 | bytes 37765120 | tf_op jit(solution)/shard_map/while/body/eval_jaxpr/hqk,hkd->hqd/dot_general | solution.py:72
  553.4 6.6 %fusion.37 = bf16[1,512,512]{2,1,0:T(8,128)(2,1)} fusion(bf16[8,512,512]{2,1,0:T(8,128)(2,1)} %add_convert_fusion, bf16[8,512,512]{2,1,0:T(8,128)(2,1)} %bitcast.102, f32[512]{0:T(512)S(1)} %convert_element_type.52), kind=kOutput, calls=%fused_computation.52 | convolution fusion | flops 2148532224 | bytes 8914944 | tf_op jit(solution)/shard_map/htd,hdc->tc/dot_general | solution.py:123
  (7 shorter events, 0.0 us)
Async XLA Ops:
  7.2 357.5 %reduce-scatter.2.cloned.1.call-start = ((), (), s32[]{:S(2)}) async-start(), calls=%async_computation.1 | async-start | bytes 25952256 | tf_op jit(solution)/shard_map/reduce_scatter | solution.py:98
  7.2 9.2 %copy-start.1 = (bf16[8,512,512]{2,1,0:T(8,128)(2,1)S(1)}, bf16[8,512,512]{2,1,0:T(8,128)(2,1)}, u32[]{:S(2)}) copy-start(bf16[8,512,512]{2,1,0:T(8,128)(2,1)} %param.17) | copy-start | bytes 12582916
  7.2 9.2 %copy-start.4 = (bf16[8,512,512]{2,1,0:T(8,128)(2,1)S(1)}, bf16[8,512,512]{2,1,0:T(8,128)(2,1)}, u32[]{:S(2)}) copy-start(bf16[8,512,512]{2,1,0:T(8,128)(2,1)} %param.11) | copy-start | bytes 12582916
  16.4 5.6 copy-start.8
  16.4 5.6 copy-start.7
  16.5 5.7 %copy-start = (bf16[8,512,512]{2,1,0:T(8,128)(2,1)S(1)}, bf16[8,512,512]{2,1,0:T(8,128)(2,1)}, u32[]{:S(2)}) copy-start(bf16[8,512,512]{2,1,0:T(8,128)(2,1)} %param.18) | copy-start | bytes 12582916
  16.5 5.7 %copy-start.5 = (bf16[8,512,512]{2,1,0:T(8,128)(2,1)S(1)}, bf16[8,512,512]{2,1,0:T(8,128)(2,1)}, u32[]{:S(2)}) copy-start(bf16[8,512,512]{2,1,0:T(8,128)(2,1)} %param.12) | copy-start | bytes 12582916
  25.0 12.9 %copy-start.2 = (f32[8,512,512]{2,1,0:T(8,128)}, f32[8,512,512]{2,1,0:T(8,128)S(1)}, u32[]{:S(2)}) copy-start(f32[8,512,512]{2,1,0:T(8,128)S(1)} %fusion.25) | copy-start | bytes 25165828
  121.0 386.0 %all-gather.2.cloned.1.call-start = ((), (), s32[]{:S(2)}) async-start(), calls=%async_computation.2 | async-start | bytes 12976128 | tf_op jit(solution)/shard_map/all_gather | solution.py:105
  121.0 252.9 %copy-start.9 = (s32[512]{0:T(512)S(1)}, s32[512]{0:T(512)}, u32[]{:S(2)}) copy-start(s32[512]{0:T(512)} %param.14) | copy-start | bytes 6148
  368.3 106.0 %collective-permute-start = (bf16[8,512,512]{2,1,0:T(8,128)(2,1)}, bf16[8,512,512]{2,1,0:T(8,128)(2,1)}, u32[]{:S(2)}, u32[]{:S(2)}) collective-permute-start(bf16[8,512,512]{2,1,0:T(8,128)(2,1)} %param.11), channel_id=1, source_target_pairs={{0,1},{1,2},{2,3},{3,4},{4,5},{5,6},{6,7},{7,8},{8,9},{9,10},{10,1... | collective-permute-start | bytes 12582920 | tf_op jit(solution)/shard_map/ppermute | solution.py:17
  370.2 168.1 %collective-permute-start.1 = (bf16[8,512,512]{2,1,0:T(8,128)(2,1)}, bf16[8,512,512]{2,1,0:T(8,128)(2,1)}, u32[]{:S(2)}, u32[]{:S(2)}) collective-permute-start(bf16[8,512,512]{2,1,0:T(8,128)(2,1)} %param.12), channel_id=1, source_target_pairs={{0,1},{1,2},{2,3},{3,4},{4,5},{5,6},{6,7},{7,8},{8,9},{9,10},{10,1... | collective-permute-start | bytes 12582920 | tf_op jit(solution)/shard_map/ppermute | solution.py:17
  507.0 14.0 %copy-start.6 = (bf16[8,512,512]{2,1,0:T(8,128)(2,1)S(1)}, bf16[8,512,512]{2,1,0:T(8,128)(2,1)}, u32[]{:S(2)}) copy-start(bf16[8,512,512]{2,1,0:T(8,128)(2,1)} %param.10) | copy-start | bytes 12582916
  516.4 4.6 copy-start.3
Sparse Core Ops, SparseCore 0:
  121.1 243.4 reduce-scatter.1
  368.5 113.1 all-gather.1
where the time goes:
time: 567 us
  waiting for transfers between devices  333 us (59%)
  matrix products  111 us (20%)
  other arithmetic  60 us (11%)
  blocking collectives  39.1 us (7%)
  between operations  14.2 us (3%)
  starting transfers between devices  5.67 us (1%)
    reduce_scatter x1, waiting for transfers between devices, local(): lax.psum_scatter(jnp.stack((term_gate, term_up, term_down), axis=2) * inn...  233 us
    ppermute x2, waiting for transfers between devices, passed_along(): return lax.ppermute(block, axis, route)  99.8 us
    psum x1, blocking collectives, local(): totals = lax.psum(rate_local, 'seq')  39.1 us
    mul x1, other arithmetic, local(): jnp.stack((term_gate, term_up, term_down), axis=2)  18 us
    sub x1, other arithmetic, attend(): expon = jnp.exp(scores - row_max)  17.5 us
    dot_general x1, matrix products, attend(): jnp.einsum('hqd,hkd->hqk', query_rows, keys_all, preferred_element_type=j...  15.1 us
    dot_general x1, matrix products, attend(): jnp.einsum('hqk,hkd->hqd', prob_bf, values_all, preferred_element_type=jn...  15 us
    dot_general x1, matrix products, local(): jnp.einsum('htr,htd->rhd', grad_up, key_rows, preferred_element_type=jnp....  13.3 us
  transfers between devices with their start and end apart: 4, of which 2 were waited for; matrix products, arithmetic and copies ran while one was open for 12% of the time, Pallas kernels for 0%

commit v1 on v0

v1 whole, which is shorter than its diff:
```python
import math

import jax
import jax.numpy as jnp
from jax import lax
from jax.sharding import PartitionSpec as P

WIN = 512


eps_norm = 1e-06


def passed_along(block, axis, distance):
    devices = range(lax.axis_size(axis))
    route = [(i - distance, i) for i in devices if i - distance in devices]
    return lax.ppermute(block, axis, route)


def renorm_rows(old_rows, summed, factor):
    old_f = old_rows.astype(jnp.float32)
    updated = old_f + summed.astype(jnp.float32) * factor[:, None]
    old_norm = jnp.sqrt(jnp.sum(old_f * old_f, axis=-1, keepdims=True))
    new_norm = jnp.sqrt(jnp.sum(updated * updated, axis=-1, keepdims=True) + eps_norm)
    return (updated * (old_norm / new_norm)).astype(jnp.bfloat16)


def half_total(rate, seq_count):
    half = seq_count // 2
    if half & (half - 1):
        in_first = lax.axis_index("seq") < half
        return lax.psum(jnp.where(in_first, rate, 0.0), "seq")
    step = 1
    while step < half:
        rate = rate + lax.ppermute(rate, "seq", [(i, i ^ step) for i in range(seq_count)])
        step *= 2
    return rate


def local(
    query_rows,
    key_rows,
    value_rows,
    step_rate,
    doc_start,
    speech_flag,
    w_gate,
    w_up,
    w_down,
    w_cond,
):
    head_local, tok_local, head_width = query_rows.shape
    cond_width = w_cond.shape[1]
    seq_count = lax.axis_size("seq")
    head_count = lax.axis_size("head")
    seq_index = lax.axis_index("seq")
    offset = seq_index * tok_local
    half_seq = seq_count // 2
    update_len = tok_local * half_seq
    in_first = seq_index < half_seq
    speech_on = speech_flag.astype(jnp.float32)
    prev_key, prev_value = passed_along((key_rows, value_rows), "seq", 1)
    score_scale = 1.0 / math.sqrt(head_width)
    groups = [list(range(half_seq)), list(range(half_seq, seq_count))]
    totals = half_total(jnp.sum(step_rate, axis=1), seq_count)

    scaled = (
        speech_on[None, :, None] * step_rate[:, :, None] * value_rows.astype(jnp.float32)
    ).astype(jnp.bfloat16)
    gate_pre = jnp.einsum("htd,hrd->htr", key_rows, w_gate, preferred_element_type=jnp.float32)
    up_pre = jnp.einsum("htd,hrd->htr", key_rows, w_up, preferred_element_type=jnp.float32)
    sigma = jax.nn.sigmoid(gate_pre)
    active = gate_pre * sigma
    hidden_zero = (active * up_pre).astype(jnp.bfloat16)
    back = jnp.einsum("htd,hdr->htr", scaled, w_down, preferred_element_type=jnp.float32)
    grad_gate = (back * up_pre * sigma * (1.0 + gate_pre * (1.0 - sigma))).astype(jnp.bfloat16)
    grad_up = (back * active).astype(jnp.bfloat16)

    flat = (head_local * head_width, head_width)
    half_index = lax.rem(seq_index, half_seq)
    share = flat[0] // half_seq

    def own_rows(rows):
        return lax.dynamic_slice_in_dim(rows, half_index * share, share, 0)

    def reduced(left, right):
        term = jnp.einsum("hta,htb->hab", left, right, preferred_element_type=jnp.float32)
        return term.astype(jnp.bfloat16).reshape(flat)

    def scattered(term):
        return lax.psum_scatter(
            term, "seq", scatter_dimension=0, axis_index_groups=groups, tiled=True
        )

    term_gate = reduced(grad_gate, key_rows)
    term_gate, prev_key, totals = lax.optimization_barrier((term_gate, prev_key, totals))
    sum_gate = scattered(term_gate)
    sum_up = scattered(reduced(grad_up, key_rows))
    term_down = reduced(scaled, hidden_zero)
    term_down, prev_value = lax.optimization_barrier((term_down, prev_value))
    sum_down = scattered(term_down)

    keys_all = jnp.concatenate([prev_key, key_rows], axis=1)
    values_all = jnp.concatenate([prev_value, value_rows], axis=1)
    pos_query = offset + jnp.arange(tok_local, dtype=jnp.int32)
    pos_key = offset - WIN + jnp.arange(WIN + tok_local, dtype=jnp.int32)
    allowed = (
        (pos_key[None, :] <= pos_query[:, None])
        & (pos_key[None, :] > pos_query[:, None] - WIN)
        & (pos_key[None, :] >= doc_start[:, None])
    )
    scores = (
        jnp.einsum("hqd,hkd->hqk", query_rows, keys_all, preferred_element_type=jnp.float32)
        * score_scale
    )
    scores = jnp.where(allowed[None], scores, -1e30)
    row_max = jnp.max(scores, axis=-1, keepdims=True)
    expon = jnp.exp(scores - row_max)
    prob_bf = (expon / jnp.sum(expon, axis=-1, keepdims=True)).astype(jnp.bfloat16)
    attended = jnp.einsum(
        "hqk,hkd->hqd", prob_bf, values_all, preferred_element_type=jnp.float32
    ).astype(jnp.bfloat16)

    sum_gate, attended = lax.optimization_barrier((sum_gate, attended))
    inner = 2.0 * update_len / (totals * math.sqrt(update_len * head_width))
    factor = own_rows(jnp.repeat(inner, head_width))

    def renewed(weight, summed):
        old = own_rows(weight.reshape(flat))
        sent = passed_along(renorm_rows(old, summed, factor), "seq", half_seq)
        return jnp.where(in_first, old, sent)

    def gathered(rows):
        whole = lax.all_gather(rows, "seq", axis=0, axis_index_groups=groups, tiled=True)
        return whole.reshape(head_local, head_width, head_width)

    rows_gate = renewed(w_gate, sum_gate)
    rows_gate, sum_up = lax.optimization_barrier((rows_gate, sum_up))
    use_gate = gathered(rows_gate)
    rows_up = renewed(w_up, sum_up)
    rows_up, sum_down = lax.optimization_barrier((rows_up, sum_down))
    use_up = gathered(rows_up)
    use_down = gathered(renewed(w_down, sum_down))

    query_gate = jnp.einsum("htd,hrd->htr", query_rows, use_gate, preferred_element_type=jnp.float32)
    query_up = jnp.einsum("htd,hrd->htr", query_rows, use_up, preferred_element_type=jnp.float32)
    query_hidden = (query_gate * jax.nn.sigmoid(query_gate) * query_up).astype(jnp.bfloat16)
    query_hidden, use_down = lax.optimization_barrier((query_hidden, use_down))
    fast_out = jnp.einsum(
        "htr,hdr->htd", query_hidden, use_down, preferred_element_type=jnp.float32
    )
    mixed = (attended + fast_out).astype(jnp.bfloat16)
    frame_rows = tok_local // head_count
    head_index = lax.axis_index("head")
    flag_rows = lax.dynamic_slice_in_dim(speech_on, head_index * frame_rows, frame_rows, 0)
    cond_weight = w_cond.reshape(head_local, head_width, cond_width)
    projected = lax.psum_scatter(
        jnp.einsum("htd,hdc->tc", mixed, cond_weight, preferred_element_type=jnp.float32).astype(
            jnp.bfloat16
        ),
        "head",
        scatter_dimension=0,
        tiled=True,
    ).astype(jnp.float32)
    cond = (projected * flag_rows[:, None]).astype(jnp.bfloat16)[None]
    return (mixed, cond)


def solution(mesh):
    placed = (
        P("head", "seq", None),
        P("head", "seq", None),
        P("head", "seq", None),
        P("head", "seq"),
        P("seq"),
        P("seq"),
        P("head", None, None),
        P("head", None, None),
        P("head", None, None),
        P("head", None),
    )
    return jax.shard_map(
        local,
        mesh=mesh,
        in_specs=placed,
        out_specs=(P("head", "seq", None), P("seq", "head", None)),
        check_vma=False,
    )
```

time: 567 us -> 441 us (0.78)
  waiting for transfers between devices: 333 us -> 262 us
  blocking collectives: 39.1 us -> 0 us
  other arithmetic: 60 us -> 32.6 us
  starting transfers between devices: 5.67 us -> 17 us
    reduce_scatter x1 -> x3, waiting for transfers between devices: 233 us -> 93.8 us  [scattered(): lax.psum_scatter(term, 'seq', scatter_dimension=0, axis_index_groups=grou...]
    all_gather x1 -> x3, waiting for transfers between devices: 0.01 us -> 75.8 us  [gathered(): lax.all_gather(rows, 'seq', axis=0, axis_index_groups=groups, tiled=True)]
    psum x1 -> x0, blocking collectives: 39.1 us -> none  [local(): totals = lax.psum(rate_local, 'seq')]
    mul x3 -> x0, other arithmetic: 18 us -> none  [the longest x1 18 us: local(): jnp.stack((term_gate, term_up, term_down), axis=2)]
    ppermute x2 -> x5, waiting for transfers between devices: 99.8 us -> 84.6 us  [passed_along(): return lax.ppermute(block, axis, route)]
    another operation x1 -> x0, other arithmetic: 10.7 us -> none  [local(): jnp.stack((w_gate, w_up, w_down), axis=2)]
    ppermute x2 -> x5, starting transfers between devices: 5.59 us -> 13.2 us  [passed_along(): return lax.ppermute(block, axis, route)]
    ppermute x0 -> x4, waiting for transfers between devices: none -> 7.3 us  [half_total(): lax.ppermute(rate, 'seq', [(i, i ^ step) for i in range(seq_count)])]
  transfers between devices with their start and end apart: 4 -> 15, of which waited for: 2 -> 13; matrix products, arithmetic and copies ran while one was open for 12% -> 30% of each run, Pallas kernels for 0% -> 0%
where the time goes in v1:
time: 441 us; the launch traced here: 438 us
  waiting for transfers between devices  262 us (59%)
  matrix products  112 us (25%)
  other arithmetic  32.6 us (7%)
  starting transfers between devices  17 us (4%)
  between operations  14.4 us (3%)
    reduce_scatter x3, waiting for transfers between devices, scattered(): lax.psum_scatter(term, 'seq', scatter_dimension=0, axis_index_groups=grou...  93.8 us
    ppermute x5, waiting for transfers between devices, passed_along(): return lax.ppermute(block, axis, route)  84.6 us
    all_gather x3, waiting for transfers between devices, gathered(): lax.all_gather(rows, 'seq', axis=0, axis_index_groups=groups, tiled=True)  75.8 us
    dot_general x3, matrix products, reduced(): jnp.einsum('hta,htb->hab', left, right, preferred_element_type=jnp.float32)  37.4 us
    sub x1, other arithmetic, local(): expon = jnp.exp(scores - row_max)  17.9 us
    dot_general x1, matrix products, local(): jnp.einsum('hqd,hkd->hqk', query_rows, keys_all, preferred_element_type=j...  15 us
    ppermute x5, starting transfers between devices, passed_along(): return lax.ppermute(block, axis, route)  13.2 us
    dot_general x1, matrix products, local(): jnp.einsum('hqk,hkd->hqd', prob_bf, values_all, preferred_element_type=jn...  12.8 us
  transfers between devices with their start and end apart: 15, of which 13 were waited for; matrix products, arithmetic and copies ran while one was open for 30% of the time, Pallas kernels for 0%

profile of v1, /device:TPU:24, one launch (start us, length us, event | category | flops | bytes accessed | tf_op | source)
XLA Modules:
  0.0 438.1 jit_solution(4531081068054578601)
XLA Ops:
  7.2 0.0 reduce-scatter.4.cloned.1.call-start
  7.2 0.7 convert_element_type.78
  7.9 0.8 fusion.45
  8.7 0.0 copy-start.4
  8.8 0.1 collective-permute-start.1
  8.8 2.8 collective-permute-start
  11.6 9.1 %fusion.48 = f32[8,512,512]{2,1,0:T(8,128)} fusion(bf16[8,512,512]{2,1,0:T(8,128)(2,1)} %param.11, bf16[8,512,512]{2,1,0:T(8,128)(2,1)} %param.16), kind=kOutput, calls=%fused_computation.82 | convolution fusion | flops 2147483648 | bytes 16777216 | tf_op jit(solution)/shard_map/htd,hrd->htr/dot_general | solution.py:70
  20.7 0.0 copy-start.3
  20.7 5.6 %fusion.47 = f32[8,512,512]{2,1,0:T(8,128)} fusion(bf16[8,512,512]{2,1,0:T(8,128)(2,1)S(1)} %copy-done.1, bf16[8,512,512]{2,1,0:T(8,128)(2,1)S(1)} %copy-done.4), kind=kOutput, calls=%fused_computation.81 | convolution fusion | flops 2147483648 | bytes 16777216 | tf_op jit(solution)/shard_map/htd,hrd->htr/dot_general | solution.py:71
  26.3 2.6 fusion.21
  29.0 12.3 %fusion.25 = bf16[8,512,512]{2,1,0:T(8,128)(2,1)} fusion(bf16[8,512,512]{2,1,0:T(8,128)(2,1)S(1)} %copy-done.1, f32[8,512,512]{2,1,0:T(8,128)} %fusion.48, f32[8,512,512]{2,1,0:T(8,128)S(1)} %fusion.21, f32[8,512,512]{2,1,0:T(8,128)} %fusion.47), kind=kOutput, calls=%fused_computation.35 | convolution fusion | flops 2170552320 | bytes 33554432 | tf_op jit(solution)/shard_map/hta,htb->hab/dot_general | solution.py:87
  41.2 1.6 collective-permute-start.2
  42.8 2.1 collective-permute-done.2
  44.9 1.5 collective-permute-start.3
  46.4 2.1 collective-permute-done.3
  48.5 0.4 collective-permute-start.4
  49.0 3.1 collective-permute-done.4
  52.1 9.0 %collective-permute-done = bf16[8,512,512]{2,1,0:T(8,128)(2,1)} collective-permute-done((bf16[8,512,512]{2,1,0:T(8,128)(2,1)}, bf16[8,512,512]{2,1,0:T(8,128)(2,1)}, u32[]{:S(2)}, u32[]{:S(2)}) %collective-permute-start) | collective-permute-done | bytes 4194336 | tf_op jit(solution)/shard_map/ppermute | solution.py:17
  61.1 0.0 reduce-scatter.4.cloned.1.call-update
  61.1 0.0 reduce-scatter.6.cloned.1.call-start
  61.1 12.1 %fusion.26 = bf16[8,512,512]{2,1,0:T(8,128)(2,1)} fusion(bf16[8,512,512]{2,1,0:T(8,128)(2,1)} %param.11, f32[8,512,512]{2,1,0:T(8,128)} %copy-done, f32[8,512,512]{2,1,0:T(8,128)} %fusion.48), kind=kOutput, calls=%fused_computation.36 | convolution fusion | flops 2162163712 | bytes 25165824 | tf_op jit(solution)/shard_map/hta,htb->hab/dot_general | solution.py:87
  73.2 0.0 reduce-scatter.6.cloned.1.call-update
  73.3 0.0 reduce-scatter.8.cloned.1.call-start
  73.3 6.3 %collective-permute-start.5 = (bf16[8,512,512]{2,1,0:T(8,128)(2,1)}, bf16[8,512,512]{2,1,0:T(8,128)(2,1)}, u32[]{:S(2)}, u32[]{:S(2)}) collective-permute-start(bf16[8,512,512]{2,1,0:T(8,128)(2,1)} %param.12), channel_id=1, source_target_pairs={{0,1},{1,2},{2,3},{3,4},{4,5},{5,6},{6,7},{7,8},{8,9},{9,10},{10,1... | collective-permute-start | bytes 12582920 | tf_op jit(solution)/shard_map/ppermute | solution.py:17
  79.6 13.0 %fusion.27 = bf16[8,512,512]{2,1,0:T(8,128)(2,1)} fusion(f32[8,512,512]{2,1,0:T(8,128)} %fusion.47, bf16[8,512,512]{2,1,0:T(8,128)(2,1)} %param.12, f32[8,512]{1,0:T(8,128)S(1)} %get-tuple-element.35, f32[8,512,512]{2,1,0:T(8,128)} %fusion.48), kind=kOutput, calls=%fused_computation.37 | convolution fusion | flops 2168455168 | bytes 25182208 | tf_op jit(solution)/shard_map/hta,htb->hab/dot_general | solution.py:87
  92.7 36.6 %collective-permute-done.5 = bf16[8,512,512]{2,1,0:T(8,128)(2,1)} collective-permute-done((bf16[8,512,512]{2,1,0:T(8,128)(2,1)}, bf16[8,512,512]{2,1,0:T(8,128)(2,1)}, u32[]{:S(2)}, u32[]{:S(2)}) %collective-permute-start.5) | collective-permute-done | bytes 4194336 | tf_op jit(solution)/shard_map/ppermute | solution.py:17
  129.2 0.0 reduce-scatter.8.cloned.1.call-update
  129.3 0.0 all-gather.4.cloned.1.call-start
  129.4 0.6 compare_and_fusion
  130.0 0.1 broadcast_bitcast_fusion
  130.1 0.1 dynamic_slice.14
  130.1 15.0 %fusion.2 = f32[8,1024,512]{2,1,0:T(8,128)} fusion(bf16[8,512,512]{2,1,0:T(8,128)(2,1)} %param.10, bf16[8,512,512]{2,1,0:T(8,128)(2,1)} %param.11, bf16[8,512,512]{2,1,0:T(8,128)(2,1)} %collective-permute-done), kind=kOutput, calls=%fused_computation.5 | convolution fusion | flops 4311744512 | bytes 29360128 | tf_op jit(solution)/shard_map/hqd,hkd->hqk/dot_general | solution.py:113
  145.1 17.9 %fusion.46 = (f32[8,512]{1,0:T(8,128)S(1)}, f32[8,512,1024]{1,2,0:T(8,128)}) fusion(f32[8,1024,512]{2,1,0:T(8,128)} %fusion.2, pred[512,1024]{0,1:T(8,128)(4,1)S(1)} %compare_and_fusion), kind=kOutput, calls=%fused_computation.80 | output fusion | flops 25166848 | bytes 34095104 | tf_op jit(solution)/shard_map/sub | solution.py:118
  163.0 12.8 %fusion.22 = bf16[8,512,512]{2,1,0:T(8,128)(2,1)} fusion(bf16[8,512,512]{2,1,0:T(8,128)(2,1)} %param.12, bf16[8,512,512]{2,1,0:T(8,128)(2,1)} %collective-permute-done.5, f32[8,512,1024]{1,2,0:T(8,128)} %get-tuple-element.37, f32[8,512]{1,0:T(8,128)S(1)} %get-tuple-element.36), kind=kOutput, calls=%fused_computation.34 | convolution fusion | flops 4322230272 | bytes 29376512 | tf_op jit(solution)/shard_map/hqk,hkd->hqd/dot_general | solution.py:120
  175.8 1.3 fusion.35
  177.0 1.2 multiply_convert_fusion.19
  178.3 1.3 collective-permute-start.6
  179.6 17.2 %collective-permute-done.6 = bf16[256,512]{1,0:T(8,128)(2,1)S(1)} collective-permute-done((bf16[256,512]{1,0:T(8,128)(2,1)S(1)}, bf16[256,512]{1,0:T(8,128)(2,1)S(1)}, u32[]{:S(2)}, u32[]{:S(2)}) %collective-permute-start.6) | collective-permute-done | bytes 262176 | tf_op jit(solution)/shard_map/ppermute | solution.py:17
  196.8 1.7 broadcast_select_fusion.2
  198.5 41.4 %reduce-scatter.6.cloned.1.call-done = bf16[256,512]{1,0:T(8,128)(2,1)} async-done(((bf16[4096,512]{1,0:T(8,128)(2,1)}), bf16[256,512]{1,0:T(8,128)(2,1)}) %reduce-scatter.6.cloned.1.call-update) | async-done | bytes 262160 | tf_op jit(solution)/shard_map/reduce_scatter | solution.py:91
  239.9 0.0 all-gather.4.cloned.1.call-update
  239.9 0.0 all-gather.6.cloned.1.call-start
  240.0 1.3 fusion.36
  241.3 1.2 multiply_convert_fusion.18
  242.5 1.3 collective-permute-start.7
  243.8 12.8 %collective-permute-done.7 = bf16[256,512]{1,0:T(8,128)(2,1)S(1)} collective-permute-done((bf16[256,512]{1,0:T(8,128)(2,1)S(1)}, bf16[256,512]{1,0:T(8,128)(2,1)S(1)}, u32[]{:S(2)}, u32[]{:S(2)}) %collective-permute-start.7) | collective-permute-done | bytes 262176 | tf_op jit(solution)/shard_map/ppermute | solution.py:17
  256.6 1.7 broadcast_select_fusion.1
  258.3 52.4 %reduce-scatter.8.cloned.1.call-done = bf16[256,512]{1,0:T(8,128)(2,1)} async-done(((bf16[4096,512]{1,0:T(8,128)(2,1)}), bf16[256,512]{1,0:T(8,128)(2,1)}) %reduce-scatter.8.cloned.1.call-update) | async-done | bytes 262160 | tf_op jit(solution)/shard_map/reduce_scatter | solution.py:91
  310.7 0.0 all-gather.6.cloned.1.call-update
  310.7 0.0 all-gather.8.cloned.1.call-start
  310.8 1.3 fusion.37
  312.0 1.2 multiply_convert_fusion.17
  313.3 1.5 collective-permute-start.8
  314.8 9.0 %collective-permute-done.8 = bf16[256,512]{1,0:T(8,128)(2,1)S(1)} collective-permute-done((bf16[256,512]{1,0:T(8,128)(2,1)S(1)}, bf16[256,512]{1,0:T(8,128)(2,1)S(1)}, u32[]{:S(2)}, u32[]{:S(2)}) %collective-permute-start.8) | collective-permute-done | bytes 262176 | tf_op jit(solution)/shard_map/ppermute | solution.py:17
  323.8 1.7 broadcast_select_fusion
  325.5 0.0 all-gather.8.cloned.1.call-update
  325.5 24.4 %all-gather.4.cloned.1.call-done = bf16[4096,512]{1,0:T(8,128)(2,1)} async-done(((bf16[256,512]{1,0:T(8,128)(2,1)}), bf16[4096,512]{1,0:T(8,128)(2,1)}) %all-gather.4.cloned.1.call-update) | async-done | bytes 4194320 | tf_op jit(solution)/shard_map/all_gather | solution.py:134
  349.9 9.1 %fusion.49 = f32[8,512,512]{1,2,0:T(8,128)} fusion(bf16[8,512,512]{2,1,0:T(8,128)(2,1)} %bitcast.83, bf16[8,512,512]{2,1,0:T(8,128)(2,1)} %param.10), kind=kOutput, calls=%fused_computation.83 | convolution fusion | flops 2147483648 | bytes 16777216 | tf_op jit(solution)/shard_map/htd,hrd->htr/dot_general | solution.py:145
  359.0 26.4 %all-gather.6.cloned.1.call-done = bf16[4096,512]{1,0:T(8,128)(2,1)} async-done(((bf16[256,512]{1,0:T(8,128)(2,1)}), bf16[4096,512]{1,0:T(8,128)(2,1)}) %all-gather.6.cloned.1.call-update) | async-done | bytes 4194320 | tf_op jit(solution)/shard_map/all_gather | solution.py:134
  385.4 10.5 %fusion.10 = bf16[8,512,512]{2,1,0:T(8,128)(2,1)} fusion(f32[8,512,512]{1,2,0:T(8,128)} %fusion.49, bf16[8,512,512]{2,1,0:T(8,128)(2,1)} %bitcast.86, bf16[8,512,512]{2,1,0:T(8,128)(2,1)} %param.10), kind=kOutput, calls=%fused_computation.14 | convolution fusion | flops 2160066560 | bytes 20971520 | tf_op jit(solution)/shard_map/htd,hrd->htr/dot_general | solution.py:146
  395.9 25.0 %all-gather.8.cloned.1.call-done = bf16[4096,512]{1,0:T(8,128)(2,1)} async-done(((bf16[256,512]{1,0:T(8,128)(2,1)}), bf16[4096,512]{1,0:T(8,128)(2,1)}) %all-gather.8.cloned.1.call-update) | async-done | bytes 4194320 | tf_op jit(solution)/shard_map/all_gather | solution.py:134
  420.9 7.2 %add_convert_fusion = bf16[8,512,512]{2,1,0:T(8,128)(2,1)S(1)} fusion(bf16[8,512,512]{2,1,0:T(8,128)(2,1)} %fusion.22, bf16[8,512,512]{2,1,0:T(8,128)(2,1)} %fusion.10, bf16[8,512,512]{2,1,0:T(8,128)(2,1)} %bitcast.87), kind=kOutput, calls=%fused_computation.20 | convolution fusion | flops 2153775104 | bytes 16777216 | tf_op jit(solution)/shard_map/htr,hdr->htd/dot_general | solution.py:149
  428.1 0.0 copy-start.9
  428.1 3.1 fusion.34
  (30 shorter events, 0.1 us)
Async XLA Ops:
  7.2 168.6 %reduce-scatter.4.cloned.1.call-start = ((), (), s32[]{:S(2)}) async-start(), calls=%async_computation.3 | async-start | bytes 4456448 | tf_op jit(solution)/shard_map/reduce_scatter | solution.py:91
  7.9 0.8 copy-start.5
  8.7 12.0 %copy-start.1 = (bf16[8,512,512]{2,1,0:T(8,128)(2,1)S(1)}, bf16[8,512,512]{2,1,0:T(8,128)(2,1)}, u32[]{:S(2)}) copy-start(bf16[8,512,512]{2,1,0:T(8,128)(2,1)} %param.11) | copy-start | bytes 12582916
  8.7 12.0 %copy-start.4 = (bf16[8,512,512]{2,1,0:T(8,128)(2,1)S(1)}, bf16[8,512,512]{2,1,0:T(8,128)(2,1)}, u32[]{:S(2)}) copy-start(bf16[8,512,512]{2,1,0:T(8,128)(2,1)} %param.17) | copy-start | bytes 12582916
  8.8 32.5 %collective-permute-start.1 = (f32[8]{0:T(128)S(1)}, f32[8]{0:T(128)S(1)}, u32[]{:S(2)}, u32[]{:S(2)}) collective-permute-start(f32[8]{0:T(128)S(1)} %get-tuple-element.34), channel_id=1, source_target_pairs={{0,1},{1,0},{2,3},{3,2},{4,5},{5,4},{6,7},{7,6},{8,9},{9,8},{10,11... | collective-permute-start | bytes 104 | tf_op jit(solution)/shard_map/ppermute | solution.py:35
  8.8 52.2 %collective-permute-start = (bf16[8,512,512]{2,1,0:T(8,128)(2,1)}, bf16[8,512,512]{2,1,0:T(8,128)(2,1)}, u32[]{:S(2)}, u32[]{:S(2)}) collective-permute-start(bf16[8,512,512]{2,1,0:T(8,128)(2,1)} %param.11), channel_id=1, source_target_pairs={{0,1},{1,2},{2,3},{3,4},{4,5},{5,6},{6,7},{7,8},{8,9},{9,10},{10,1... | collective-permute-start | bytes 12582920 | tf_op jit(solution)/shard_map/ppermute | solution.py:17
  20.7 5.6 %copy-start.2 = (bf16[8,512,512]{2,1,0:T(8,128)(2,1)S(1)}, bf16[8,512,512]{2,1,0:T(8,128)(2,1)}, u32[]{:S(2)}) copy-start(bf16[8,512,512]{2,1,0:T(8,128)(2,1)} %param.18) | copy-start | bytes 12582916
  20.7 5.6 %copy-start.3 = (bf16[8,512,512]{2,1,0:T(8,128)(2,1)S(1)}, bf16[8,512,512]{2,1,0:T(8,128)(2,1)}, u32[]{:S(2)}) copy-start(bf16[8,512,512]{2,1,0:T(8,128)(2,1)} %param.12) | copy-start | bytes 12582916
  29.0 12.3 %copy-start = (f32[8,512,512]{2,1,0:T(8,128)}, f32[8,512,512]{2,1,0:T(8,128)S(1)}, u32[]{:S(2)}) copy-start(f32[8,512,512]{2,1,0:T(8,128)S(1)} %fusion.21) | copy-start | bytes 25165828
  41.2 3.7 collective-permute-start.2
  44.9 3.6 collective-permute-start.3
  48.5 3.5 collective-permute-start.4
  61.1 178.8 %reduce-scatter.6.cloned.1.call-start = ((), (), s32[]{:S(2)}) async-start(), calls=%async_computation.4 | async-start | bytes 4456448 | tf_op jit(solution)/shard_map/reduce_scatter | solution.py:91
  73.3 237.4 %reduce-scatter.8.cloned.1.call-start = ((), (), s32[]{:S(2)}) async-start(), calls=%async_computation.6 | async-start | bytes 4456448 | tf_op jit(solution)/shard_map/reduce_scatter | solution.py:91
  73.3 55.9 %collective-permute-start.5 = (bf16[8,512,512]{2,1,0:T(8,128)(2,1)}, bf16[8,512,512]{2,1,0:T(8,128)(2,1)}, u32[]{:S(2)}, u32[]{:S(2)}) collective-permute-start(bf16[8,512,512]{2,1,0:T(8,128)(2,1)} %param.12), channel_id=1, source_target_pairs={{0,1},{1,2},{2,3},{3,4},{4,5},{5,6},{6,7},{7,8},{8,9},{9,10},{10,1... | collective-permute-start | bytes 12582920 | tf_op jit(solution)/shard_map/ppermute | solution.py:17
  92.7 36.7 %copy-start.7 = (s32[512]{0:T(512)S(1)}, s32[512]{0:T(512)}, u32[]{:S(2)}) copy-start(s32[512]{0:T(512)} %param.14) | copy-start | bytes 6148
  129.3 220.6 %all-gather.4.cloned.1.call-start = ((), (), s32[]{:S(2)}) async-start(), calls=%async_computation.5 | async-start | bytes 4456448 | tf_op jit(solution)/shard_map/all_gather | solution.py:134
  178.3 18.5 %collective-permute-start.6 = (bf16[256,512]{1,0:T(8,128)(2,1)S(1)}, bf16[256,512]{1,0:T(8,128)(2,1)S(1)}, u32[]{:S(2)}, u32[]{:S(2)}) collective-permute-start(bf16[256,512]{1,0:T(8,128)(2,1)S(1)} %multiply_convert_fusion.19), channel_id=1, source_target_pairs={{0,16},{1,17},{2,18},{3,19},{4,20},{5,21},{6,22},{7,23},{8,24},{9,... | collective-permute-start | bytes 786440 | tf_op jit(solution)/shard_map/ppermute | solution.py:17
  239.9 145.5 %all-gather.6.cloned.1.call-start = ((), (), s32[]{:S(2)}) async-start(), calls=%async_computation.7 | async-start | bytes 4456448 | tf_op jit(solution)/shard_map/all_gather | solution.py:134
  242.5 14.1 %collective-permute-start.7 = (bf16[256,512]{1,0:T(8,128)(2,1)S(1)}, bf16[256,512]{1,0:T(8,128)(2,1)S(1)}, u32[]{:S(2)}, u32[]{:S(2)}) collective-permute-start(bf16[256,512]{1,0:T(8,128)(2,1)S(1)} %multiply_convert_fusion.18), channel_id=1, source_target_pairs={{0,16},{1,17},{2,18},{3,19},{4,20},{5,21},{6,22},{7,23},{8,24},{9,... | collective-permute-start | bytes 786440 | tf_op jit(solution)/shard_map/ppermute | solution.py:17
  310.7 110.2 %all-gather.8.cloned.1.call-start = ((), (), s32[]{:S(2)}) async-start(), calls=%async_computation.8 | async-start | bytes 4456448 | tf_op jit(solution)/shard_map/all_gather | solution.py:134
  313.3 10.5 %collective-permute-start.8 = (bf16[256,512]{1,0:T(8,128)(2,1)S(1)}, bf16[256,512]{1,0:T(8,128)(2,1)S(1)}, u32[]{:S(2)}, u32[]{:S(2)}) collective-permute-start(bf16[256,512]{1,0:T(8,128)(2,1)S(1)} %multiply_convert_fusion.17), channel_id=1, source_target_pairs={{0,16},{1,17},{2,18},{3,19},{4,20},{5,21},{6,22},{7,23},{8,24},{9,... | collective-permute-start | bytes 786440 | tf_op jit(solution)/shard_map/ppermute | solution.py:17
  420.9 7.2 %copy-start.6 = (f32[512]{0:T(512)S(1)}, f32[512]{0:T(512)}, u32[]{:S(2)}) copy-start(f32[512]{0:T(512)} %copy-done.5) | copy-start | bytes 6148
  420.9 7.2 %copy-start.8 = (bf16[4096,512]{1,0:T(8,128)(2,1)S(1)}, bf16[4096,512]{1,0:T(8,128)(2,1)}, u32[]{:S(2)}) copy-start(bf16[4096,512]{1,0:T(8,128)(2,1)} %param.19) | copy-start | bytes 12582916
  428.1 3.2 copy-start.9
Sparse Core Ops, SparseCore 0:
  61.2 109.0 reduce-scatter.3
  172.6 67.2 reduce-scatter.5
  242.2 68.4 reduce-scatter.7
  312.7 37.1 all-gather.3
  351.3 34.0 all-gather.5
  386.9 34.0 all-gather.7
